TPU v7x, 128 devices: a whole 4x4x4 slice. The times are simulated.
128 devices in a mesh: row: 8 (over y, core), col: 16 (over z, x).
Axes of the slice: x: 4, y: 4, z: 4, core: 2. Of those that a mesh axis runs over, the one named last changes fastest.
Arguments:
- inputs: bfloat16 [1280, 6144], P('col', 'row'), may hold values from -6 to 6
- w_in: bfloat16 [6144, 24576], P('row', 'col'), may hold values from -0.078125 to 0.078125
- b_in: float32 [24576], P('col'), may hold values from -3 to 3
- w_out: bfloat16 [24576, 6144], P('col', 'row'), may hold values from -0.0390625 to 0.0390625
- b_out: float32 [6144], P('row'), may hold values from -3 to 3
- out_grad: bfloat16 [1280, 6144], P('col', 'row'), may hold values from -0.625 to 0.625
Outputs:
- output: bfloat16 [1280, 6144], P('col', 'row')
- input_grad: bfloat16 [1280, 6144], P('col', 'row')
- w_in_grad: float32 [6144, 24576], P('row', 'col')
- b_in_grad: float32 [24576], P('col')
- w_out_grad: float32 [24576, 6144], P('col', 'row')
- b_out_grad: float32 [6144], P('row')
All inputs are finite; a program needn't handle non-finite values.
Results may differ from a plain program's by a relative error of at most 0.007.
Values may be sent and summed in bfloat16 or wider, within the bound.
A program may use at most 128 MiB of HBM per device.

v0:
```python
import jax
import jax.numpy as jnp
from jax import lax
from jax.sharding import PartitionSpec as P


def gelu_parts(hidden):
    half = 0.5 * (1.0 + jax.scipy.special.erf(hidden * 0.7071067811865476))
    slope = half + hidden * jnp.exp(-0.5 * hidden * hidden) * 0.3989422804014327
    return (hidden * half, slope)


def shards(inputs, w_in, b_in, w_out, b_out, out_grad):
    inputs_all, grad_all = (
        lax.all_gather(inputs, "col", axis=0, tiled=True),
        lax.all_gather(out_grad, "col", axis=0, tiled=True),
    )
    partial_value = jnp.dot(inputs_all, w_in, preferred_element_type=jnp.float32)
    hidden = lax.psum(partial_value, "row") + b_in
    act, slope = gelu_parts(hidden)
    act_all = act.astype(jnp.bfloat16)
    rows = act_all
    output = (
        lax.psum_scatter(
            jnp.dot(rows, w_out, preferred_element_type=jnp.float32),
            "col",
            scatter_dimension=0,
            tiled=True,
        )
        + b_out
    ).astype(jnp.bfloat16)
    b_out_grad = jnp.sum(grad_all, axis=0, dtype=jnp.float32)
    w_out_grad = jnp.einsum("tf,td->fd", act_all, grad_all, preferred_element_type=jnp.float32)
    partial_grad = jnp.einsum("td,fd->tf", grad_all, w_out, preferred_element_type=jnp.float32)
    act_grad = lax.psum(partial_grad, "row")
    pre_grad = (act_grad * slope).astype(jnp.bfloat16)
    b_in_grad = jnp.sum(pre_grad, axis=0, dtype=jnp.float32)
    w_in_grad = jnp.einsum("td,tf->df", inputs_all, pre_grad, preferred_element_type=jnp.float32)
    rows = pre_grad
    input_grad = lax.psum_scatter(
        jnp.einsum("tf,df->td", rows, w_in, preferred_element_type=jnp.float32),
        "col",
        scatter_dimension=0,
        tiled=True,
    ).astype(jnp.bfloat16)
    return (output, input_grad, w_in_grad, b_in_grad, w_out_grad, b_out_grad)


def solution(mesh):
    placed = (
        P("col", "row"),
        P("row", "col"),
        P("col"),
        P("col", "row"),
        P("row"),
        P("col", "row"),
    )
    return jax.shard_map(
        shards,
        mesh=mesh,
        in_specs=placed,
        out_specs=(
            P("col", "row"),
            P("col", "row"),
            P("row", "col"),
            P("col"),
            P("col", "row"),
            P("row"),
        ),
        check_vma=False,
    )
```

profile of v0, /device:TPU:0, one launch (start us, length us, event | category | flops | bytes accessed | tf_op | source)
XLA Modules:
  0.0 465.8 jit_solution(393771307948937727)
XLA Ops:
  7.2 0.0 copy-start
  7.2 0.0 all-gather.5.cloned.1.call-start
  7.2 0.7 all-gather.5.cloned.1.call-update
  7.9 0.0 all-gather.3.cloned.1.call-start
  8.0 0.7 all-gather.3.cloned.1.call-update
  8.7 0.0 all-reduce.3.cloned.1.call-start
  8.7 48.7 %all-gather.5.cloned.1.call-done = bf16[1280,768]{1,0:T(8,128)(2,1)} async-done(((bf16[80,768]{1,0:T(8,128)(2,1)}), bf16[1280,768]{1,0:T(8,128)(2,1)}) %all-gather.5.cloned.1.call-update) | async-done | bytes 1966096 | tf_op jit(solution)/shard_map/all_gather | solution.py:16
  57.4 8.7 %fusion.9 = f32[1280,1536]{1,0:T(8,128)} fusion(bf16[1280,768]{1,0:T(8,128)(2,1)} %all-gather.5.cloned.1.call-done, bf16[1536,768]{1,0:T(8,128)(2,1)} %param.9), kind=kOutput, calls=%fused_computation.15 | convolution fusion | flops 3019898880 | bytes 12189696 | tf_op jit(solution)/shard_map/td,fd->tf/dot_general | solution.py:34
  66.1 37.5 %all-gather.3.cloned.1.call-done = bf16[1280,768]{1,0:T(8,128)(2,1)} async-done(((bf16[80,768]{1,0:T(8,128)(2,1)}), bf16[1280,768]{1,0:T(8,128)(2,1)}) %all-gather.3.cloned.1.call-update) | async-done | bytes 1966096 | tf_op jit(solution)/shard_map/all_gather | solution.py:15
  103.5 7.0 %fusion.7 = f32[1280,1536]{1,0:T(8,128)} fusion(bf16[1280,768]{1,0:T(8,128)(2,1)} %all-gather.3.cloned.1.call-done, bf16[768,1536]{1,0:T(8,128)(2,1)S(1)} %copy-done), kind=kOutput, calls=%fused_computation.13 | convolution fusion | flops 3019898880 | bytes 12189696 | tf_op jit(solution)/shard_map/dot_general | solution.py:18
  110.5 0.0 all-reduce.3.cloned.1.call-update
  110.5 0.0 reduce-scatter.5.cloned.1.call-start
  110.6 173.0 %all-reduce.3.cloned.1.call-done = (f32[1280,1536]{1,0:T(8,128)}, f32[1280,1536]{1,0:T(8,128)}) async-done(((f32[1280,1536]{1,0:T(8,128)}, f32[1280,1536]{1,0:T(8,128)}), (f32[1280,1536]{1,0:T(8,128)}, f32[1280,1536]{1,0:T(8,128)})) %all-reduce.3.cloned.1.call-update) | async-done | bytes 15728656 | tf_op jit(solution)/shard_map/psum | solution.py:19
  283.6 0.0 copy-done.4
  283.6 10.6 %convert_reduce_fusion = (f32[1536]{0:T(1024)}, bf16[1280,1536]{1,0:T(8,128)(2,1)S(1)}, bf16[1280,1536]{1,0:T(8,128)(2,1)}) fusion(f32[1280,1536]{1,0:T(8,128)} %get-tuple-element.13, f32[1280,1536]{1,0:T(8,128)} %get-tuple-element.12, f32[1536]{0:T(1024)S(1)} %copy-done.4), kind=kLoop, calls=%fused_computation.7 | loop fusion | flops 29489664 | bytes 23605248 | tf_op jit(solution)/shard_map/reduce_sum | solution.py:37
  294.2 1.9 copy-done.2
  296.1 5.1 %fusion.10 = f32[1280,768]{1,0:T(8,128)} fusion(bf16[1280,1536]{1,0:T(8,128)(2,1)S(1)} %get-tuple-element.15, bf16[768,1536]{1,0:T(8,128)(2,1)S(1)} %copy-done), kind=kOutput, calls=%fused_computation.16 | convolution fusion | flops 3019898880 | bytes 10223616 | tf_op jit(solution)/shard_map/tf,df->td/dot_general | solution.py:41
  301.2 0.0 reduce-scatter.5.cloned.1.call-update
  301.3 0.2 reduce-scatter.3.cloned.1.call-start
  301.5 1.4 copy-done.6
  302.9 7.2 %fusion.8 = f32[1280,768]{1,0:T(8,128)} fusion(bf16[1280,1536]{1,0:T(8,128)(2,1)} %get-tuple-element.16, bf16[1536,768]{1,0:T(8,128)(2,1)S(1)} %copy-done.6), kind=kOutput, calls=%fused_computation.14 | convolution fusion | flops 3019898880 | bytes 10223616 | tf_op jit(solution)/shard_map/dot_general | solution.py:25
  310.1 0.0 reduce-scatter.3.cloned.1.call-update
  310.1 1.6 copy-done.3
  311.7 0.9 convert_reduce_fusion.1
  312.6 8.2 %convolution_bitcast_fusion = f32[768,1536]{0,1:T(8,128)} fusion(bf16[1280,1536]{1,0:T(8,128)(2,1)} %copy-done.2, bf16[1280,768]{1,0:T(8,128)(2,1)} %all-gather.3.cloned.1.call-done), kind=kOutput, calls=%fused_computation.11 | convolution fusion | flops 3019898880 | bytes 10616832 | tf_op jit(solution)/shard_map/td,tf->df/dot_general | solution.py:38
  320.8 6.1 %copy.12 = f32[768,1536]{1,0:T(8,128)} copy(f32[768,1536]{0,1:T(8,128)} %convolution_bitcast_fusion) | data formatting | bytes 9437184
  327.0 8.4 %fusion.11 = f32[1536,768]{1,0:T(8,128)} fusion(bf16[1280,1536]{1,0:T(8,128)(2,1)} %get-tuple-element.16, bf16[1280,768]{1,0:T(8,128)(2,1)} %all-gather.5.cloned.1.call-done), kind=kOutput, calls=%fused_computation.17 | convolution fusion | flops 3019898880 | bytes 10616832 | tf_op jit(solution)/shard_map/tf,td->fd/dot_general | solution.py:33
  335.4 42.9 %reduce-scatter.5.cloned.1.call-done = f32[80,768]{1,0:T(8,128)} async-done(((f32[1280,768]{1,0:T(8,128)}), f32[80,768]{1,0:T(8,128)}) %reduce-scatter.5.cloned.1.call-update) | async-done | bytes 245776 | tf_op jit(solution)/shard_map/reduce_scatter | solution.py:40
  378.3 1.6 convert_element_type.21
  379.9 77.8 %reduce-scatter.3.cloned.1.call-done = f32[80,768]{1,0:T(8,128)} async-done(((f32[1280,768]{1,0:T(8,128)}), f32[80,768]{1,0:T(8,128)}) %reduce-scatter.3.cloned.1.call-update) | async-done | bytes 245776 | tf_op jit(solution)/shard_map/reduce_scatter | solution.py:24
  457.7 0.0 copy-done.5
  457.7 1.6 add_convert_fusion
  (8 shorter events, 0.0 us)
Async XLA Ops:
  7.2 96.4 %copy-start = (bf16[768,1536]{1,0:T(8,128)(2,1)S(1)}, bf16[768,1536]{1,0:T(8,128)(2,1)}, u32[]{:S(2)}) copy-start(bf16[768,1536]{1,0:T(8,128)(2,1)} %param.7) | copy-start | bytes 7077892
  7.2 50.2 %all-gather.5.cloned.1.call-start = ((), (), s32[]{:S(2)}) async-start(), calls=%async_computation.4 | async-start | bytes 2088960 | tf_op jit(solution)/shard_map/all_gather | solution.py:16
  7.9 95.6 %all-gather.3.cloned.1.call-start = ((), (), s32[]{:S(2)}) async-start(), calls=%async_computation.2 | async-start | bytes 2088960 | tf_op jit(solution)/shard_map/all_gather | solution.py:15
  8.7 274.9 %all-reduce.3.cloned.1.call-start = ((), (), s32[]{:S(2)}) async-start(), calls=%async_computation.6 | async-start | bytes 31457280 | tf_op jit(solution)/shard_map/psum | solution.py:19
  110.5 173.1 %copy-start.4 = (f32[1536]{0:T(1024)S(1)}, f32[1536]{0:T(1024)}, u32[]{:S(2)}) copy-start(f32[1536]{0:T(1024)} %param.8) | copy-start | bytes 18436
  110.5 267.7 %reduce-scatter.5.cloned.1.call-start = ((), (), s32[]{:S(2)}) async-start(), calls=%async_computation.5 | async-start | bytes 4177920 | tf_op jit(solution)/shard_map/reduce_scatter | solution.py:40
  294.2 1.9 copy-start.2
  301.2 1.7 copy-start.6
  301.3 156.4 %reduce-scatter.3.cloned.1.call-start = ((), (), s32[]{:S(2)}) async-start(), calls=%async_computation.3 | async-start | bytes 4177920 | tf_op jit(solution)/shard_map/reduce_scatter | solution.py:24
  310.1 1.6 copy-start.3
  327.0 130.7 %copy-start.5 = (f32[768]{0:T(1024)S(1)}, f32[768]{0:T(1024)}, u32[]{:S(2)}) copy-start(f32[768]{0:T(1024)} %param.10) | copy-start | bytes 9220
  327.0 132.3 %copy-start.1 = (bf16[768,1536]{1,0:T(8,128)(2,1)S(1)}, bf16[768,1536]{1,0:T(8,128)(2,1)}, u32[]{:S(2)}) copy-start(bf16[768,1536]{1,0:T(8,128)(2,1)} %param.7) | copy-start | bytes 7077892
Sparse Core Ops, SparseCore 0:
  10.2 47.1 all-gather.4
  59.5 43.9 all-gather.2
  110.6 172.8 all-reduce.2
  301.4 76.8 reduce-scatter.4
  381.5 76.1 reduce-scatter.2
where the time goes:
time: 466 us
  waiting for transfers between devices  381 us (82%)
  matrix products  44.6 us (10%)
  other arithmetic  14.7 us (3%)
  between operations  13.8 us (3%)
  local copies, waits for them, and re-layouts  11 us (2%)
    psum x1, waiting for transfers between devices, shards(): hidden = lax.psum(partial_value, 'row') + b_in  173 us
    reduce_scatter x1, waiting for transfers between devices, shards(): lax.psum_scatter(jnp.dot(rows, w_out, preferred_element_type=jnp.float32)...  77.8 us
    all_gather x1, waiting for transfers between devices, shards(): lax.all_gather(out_grad, 'col', axis=0, tiled=True)  48.7 us
    reduce_scatter x1, waiting for transfers between devices, shards(): lax.psum_scatter(jnp.einsum('tf,df->td', rows, w_in, preferred_element_ty...  42.9 us
    all_gather x1, waiting for transfers between devices, shards(): lax.all_gather(inputs, 'col', axis=0, tiled=True)  37.5 us
    unnamed x15, local copies, waits for them, and re-layouts  11 us
    reduce_sum x1, other arithmetic, shards(): b_in_grad = jnp.sum(pre_grad, axis=0, dtype=jnp.float32)  10.6 us
  transfers between devices with their start and end apart: 5, of which 5 were waited for; matrix products, arithmetic and copies ran while one was open for 9% of the time, Pallas kernels for 0%

commit v1 on v0

--- a/solution.py
+++ b/solution.py
@@ -1,7 +1,15 @@
+import functools
 import jax
 import jax.numpy as jnp
 from jax import lax
 from jax.sharding import PartitionSpec as P
+
+
+def rounds_create(shard_in, row_axis):
+    return jnp.sum(lax.all_gather(shard_in, row_axis), axis=0)
+
+
+pack_the_column = functools.partial(rounds_create, row_axis="row")
 
 
 def gelu_parts(hidden):
@@ -16,7 +24,7 @@
         lax.all_gather(out_grad, "col", axis=0, tiled=True),
     )
     partial_value = jnp.dot(inputs_all, w_in, preferred_element_type=jnp.float32)
-    hidden = lax.psum(partial_value, "row") + b_in
+    hidden = pack_the_column(partial_value) + b_in
     act, slope = gelu_parts(hidden)
     act_all = act.astype(jnp.bfloat16)
     rows = act_all

time: 466 us -> 668 us (1.43)
  waiting for transfers between devices: 381 us -> 558 us
  other arithmetic: 14.7 us -> 39.4 us
    all_gather x0 -> x1, waiting for transfers between devices: none -> 271 us  [rounds_create(): return jnp.sum(lax.all_gather(shard_in, row_axis), axis=0)]
    psum x1, waiting for transfers between devices: 173 us -> 77.1 us  [shards(): act_grad = lax.psum(partial_grad, 'row')]
    reduce_sum x0 -> x1, other arithmetic: none -> 24.7 us  [rounds_create(): return jnp.sum(lax.all_gather(shard_in, row_axis), axis=0)]
    all_gather x1, waiting for transfers between devices: 37.5 us -> 48.7 us  [shards(): lax.all_gather(inputs, 'col', axis=0, tiled=True)]
    all_gather x1, waiting for transfers between devices: 48.7 us -> 39.1 us  [shards(): lax.all_gather(out_grad, 'col', axis=0, tiled=True)]
  transfers between devices with their start and end apart: 5 -> 6, of which waited for: 5 -> 6; matrix products, arithmetic and copies ran while one was open for 9% -> 11% of each run, Pallas kernels for 0% -> 0%
where the time goes in v1:
time: 668 us
  waiting for transfers between devices  558 us (84%)
  matrix products  44.5 us (7%)
  other arithmetic  39.4 us (6%)
  between operations  14.1 us (2%)
  local copies, waits for them, and re-layouts  11 us (2%)
    all_gather x1, waiting for transfers between devices, rounds_create(): return jnp.sum(lax.all_gather(shard_in, row_axis), axis=0)  271 us
    reduce_scatter x1, waiting for transfers between devices, shards(): lax.psum_scatter(jnp.dot(rows, w_out, preferred_element_type=jnp.float32)...  77.9 us
    psum x1, waiting for transfers between devices, shards(): act_grad = lax.psum(partial_grad, 'row')  77.1 us
    all_gather x1, waiting for transfers between devices, shards(): lax.all_gather(inputs, 'col', axis=0, tiled=True)  48.7 us
    reduce_scatter x1, waiting for transfers between devices, shards(): lax.psum_scatter(jnp.einsum('tf,df->td', rows, w_in, preferred_element_ty...  42.8 us
    all_gather x1, waiting for transfers between devices, shards(): lax.all_gather(out_grad, 'col', axis=0, tiled=True)  39.1 us
    reduce_sum x1, other arithmetic, rounds_create(): return jnp.sum(lax.all_gather(shard_in, row_axis), axis=0)  24.7 us
  transfers between devices with their start and end apart: 6, of which 6 were waited for; matrix products, arithmetic and copies ran while one was open for 11% of the time, Pallas kernels for 0%

profile of v1, /device:TPU:0, one launch (start us, length us, event | category | flops | bytes accessed | tf_op | source)
XLA Modules:
  0.0 668.0 jit_solution(8866211675892188899)
XLA Ops:
  7.2 0.0 all-gather.5.cloned.1.call-start
  7.2 0.7 all-gather.5.cloned.1.call-update
  7.9 0.0 all-gather.7.cloned.1.call-start
  8.0 0.7 all-gather.7.cloned.1.call-update
  8.7 0.0 all-gather.9.cloned.1.call-start
  8.7 48.7 %all-gather.5.cloned.1.call-done = bf16[1280,768]{1,0:T(8,128)(2,1)} async-done(((bf16[80,768]{1,0:T(8,128)(2,1)}), bf16[1280,768]{1,0:T(8,128)(2,1)}) %all-gather.5.cloned.1.call-update) | async-done | bytes 1966096 | tf_op jit(solution)/shard_map/all_gather | solution.py:23
  57.4 7.0 %fusion.7 = f32[1280,1536]{1,0:T(8,128)} fusion(bf16[1280,768]{1,0:T(8,128)(2,1)} %all-gather.5.cloned.1.call-done, bf16[768,1536]{1,0:T(8,128)(2,1)S(1)} %copy-done), kind=kOutput, calls=%fused_computation.13 | convolution fusion | flops 3019898880 | bytes 12189696 | tf_op jit(solution)/shard_map/dot_general | solution.py:26
  64.3 0.0 all-gather.9.cloned.1.call-update
  64.4 0.0 all-reduce.2.cloned.1.call-start
  64.4 39.1 %all-gather.7.cloned.1.call-done = bf16[1280,768]{1,0:T(8,128)(2,1)} async-done(((bf16[80,768]{1,0:T(8,128)(2,1)}), bf16[1280,768]{1,0:T(8,128)(2,1)}) %all-gather.7.cloned.1.call-update) | async-done | bytes 1966096 | tf_op jit(solution)/shard_map/all_gather | solution.py:24
  103.5 8.6 %fusion.9 = f32[1280,1536]{1,0:T(8,128)} fusion(bf16[1280,768]{1,0:T(8,128)(2,1)} %all-gather.7.cloned.1.call-done, bf16[1536,768]{1,0:T(8,128)(2,1)} %param.9), kind=kOutput, calls=%fused_computation.15 | convolution fusion | flops 3019898880 | bytes 12189696 | tf_op jit(solution)/shard_map/td,fd->tf/dot_general | solution.py:42
  112.1 0.0 all-reduce.2.cloned.1.call-update
  112.2 0.0 reduce-scatter.5.cloned.1.call-start
  112.2 271.4 %all-gather.9.cloned.1.call-done = f32[10240,1536]{1,0:T(8,128)} async-done(((f32[1280,1536]{1,0:T(8,128)}), f32[10240,1536]{1,0:T(8,128)}) %all-gather.9.cloned.1.call-update) | async-done | bytes 62914576 | tf_op jit(solution)/shard_map/all_gather | solution.py:9
  383.6 24.7 %reduce_sum.27 = f32[1280,1536]{1,0:T(8,128)} reduce(f32[8,1280,1536]{2,1,0:T(8,128)} %bitcast.15, f32[]{:T(128)} %constant.0.clone.1), dimensions={0}, to_apply=%region_0.0 | reduce | flops 13762560 | bytes 70778880 | tf_op jit(solution)/shard_map/reduce_sum | solution.py:9
  408.3 77.1 %all-reduce.2.cloned.1.call-done = f32[1280,1536]{1,0:T(8,128)} async-done(((f32[1280,1536]{1,0:T(8,128)}), f32[1280,1536]{1,0:T(8,128)}) %all-reduce.2.cloned.1.call-update) | async-done | bytes 7864336 | tf_op jit(solution)/shard_map/psum | solution.py:43
  485.4 10.6 %convert_reduce_fusion = (f32[1536]{0:T(1024)}, bf16[1280,1536]{1,0:T(8,128)(2,1)S(1)}, bf16[1280,1536]{1,0:T(8,128)(2,1)}) fusion(f32[1280,1536]{1,0:T(8,128)} %all-reduce.2.cloned.1.call-done, f32[1280,1536]{1,0:T(8,128)} %reduce_sum.27, f32[1536]{0:T(1024)S(1)} %copy-done.4), kind=kLoop, calls=%fused_computation.7 | loop fusion | flops 29489664 | bytes 23605248 | tf_op jit(solution)/shard_map/reduce_sum | solution.py:45
  496.0 1.9 copy-done.2
  497.9 5.1 fusion.10
  503.0 0.0 reduce-scatter.5.cloned.1.call-update
  503.1 0.2 reduce-scatter.3.cloned.1.call-start
  503.3 1.4 copy-done.6
  504.7 7.2 %fusion.8 = f32[1280,768]{1,0:T(8,128)} fusion(bf16[1280,1536]{1,0:T(8,128)(2,1)} %get-tuple-element.14, bf16[1536,768]{1,0:T(8,128)(2,1)S(1)} %copy-done.6), kind=kOutput, calls=%fused_computation.14 | convolution fusion | flops 3019898880 | bytes 10223616 | tf_op jit(solution)/shard_map/dot_general | solution.py:33
  511.9 1.6 copy-done.3
  513.5 0.9 convert_reduce_fusion.1
  514.4 8.2 %convolution_bitcast_fusion = f32[768,1536]{0,1:T(8,128)} fusion(bf16[1280,1536]{1,0:T(8,128)(2,1)} %copy-done.2, bf16[1280,768]{1,0:T(8,128)(2,1)} %all-gather.5.cloned.1.call-done), kind=kOutput, calls=%fused_computation.11 | convolution fusion | flops 3019898880 | bytes 10616832 | tf_op jit(solution)/shard_map/td,tf->df/dot_general | solution.py:46
  522.6 6.1 copy.12
  528.7 8.4 %fusion.11 = f32[1536,768]{1,0:T(8,128)} fusion(bf16[1280,1536]{1,0:T(8,128)(2,1)} %get-tuple-element.14, bf16[1280,768]{1,0:T(8,128)(2,1)} %all-gather.7.cloned.1.call-done), kind=kOutput, calls=%fused_computation.17 | convolution fusion | flops 3019898880 | bytes 10616832 | tf_op jit(solution)/shard_map/tf,td->fd/dot_general | solution.py:41
  537.2 42.8 %reduce-scatter.5.cloned.1.call-done = f32[80,768]{1,0:T(8,128)} async-done(((f32[1280,768]{1,0:T(8,128)}), f32[80,768]{1,0:T(8,128)}) %reduce-scatter.5.cloned.1.call-update) | async-done | bytes 245776 | tf_op jit(solution)/shard_map/reduce_scatter | solution.py:48
  580.0 1.6 convert_element_type.21
  581.6 77.9 %reduce-scatter.3.cloned.1.call-done = f32[80,768]{1,0:T(8,128)} async-done(((f32[1280,768]{1,0:T(8,128)}), f32[80,768]{1,0:T(8,128)}) %reduce-scatter.3.cloned.1.call-update) | async-done | bytes 245776 | tf_op jit(solution)/shard_map/reduce_scatter | solution.py:32
  659.5 1.6 add_convert_fusion
  (12 shorter events, 0.0 us)
Async XLA Ops:
  7.2 50.2 %copy-start = (bf16[768,1536]{1,0:T(8,128)(2,1)S(1)}, bf16[768,1536]{1,0:T(8,128)(2,1)}, u32[]{:S(2)}) copy-start(bf16[768,1536]{1,0:T(8,128)(2,1)} %param.7) | copy-start | bytes 7077892
  7.2 50.2 %all-gather.5.cloned.1.call-start = ((), (), s32[]{:S(2)}) async-start(), calls=%async_computation.2 | async-start | bytes 2088960 | tf_op jit(solution)/shard_map/all_gather | solution.py:23
  7.9 95.6 %all-gather.7.cloned.1.call-start = ((), (), s32[]{:S(2)}) async-start(), calls=%async_computation.4 | async-start | bytes 2088960 | tf_op jit(solution)/shard_map/all_gather | solution.py:24
  8.7 374.9 %all-gather.9.cloned.1.call-start = ((), (), s32[]{:S(2)}) async-start(), calls=%async_computation.7 | async-start | bytes 70778880 | tf_op jit(solution)/shard_map/all_gather | solution.py:9
  64.4 421.0 %all-reduce.2.cloned.1.call-start = ((), (), s32[]{:S(2)}) async-start(), calls=%async_computation.5 | async-start | bytes 15728640 | tf_op jit(solution)/shard_map/psum | solution.py:43
  112.2 467.8 %reduce-scatter.5.cloned.1.call-start = ((), (), s32[]{:S(2)}) async-start(), calls=%async_computation.6 | async-start | bytes 4177920 | tf_op jit(solution)/shard_map/reduce_scatter | solution.py:48
  383.6 101.8 %copy-start.4 = (f32[1536]{0:T(1024)S(1)}, f32[1536]{0:T(1024)}, u32[]{:S(2)}) copy-start(f32[1536]{0:T(1024)} %param.8) | copy-start | bytes 18436
  496.0 1.9 copy-start.2
  503.0 1.7 copy-start.6
  503.1 156.4 %reduce-scatter.3.cloned.1.call-start = ((), (), s32[]{:S(2)}) async-start(), calls=%async_computation.3 | async-start | bytes 4177920 | tf_op jit(solution)/shard_map/reduce_scatter | solution.py:32
  511.9 1.6 copy-start.3
  528.7 130.8 %copy-start.5 = (f32[768]{0:T(1024)S(1)}, f32[768]{0:T(1024)}, u32[]{:S(2)}) copy-start(f32[768]{0:T(1024)} %param.10) | copy-start | bytes 9220
  528.7 132.4 %copy-start.1 = (bf16[768,1536]{1,0:T(8,128)(2,1)S(1)}, bf16[768,1536]{1,0:T(8,128)(2,1)}, u32[]{:S(2)}) copy-start(bf16[768,1536]{1,0:T(8,128)(2,1)} %param.7) | copy-start | bytes 7077892
Sparse Core Ops, SparseCore 0:
  10.2 47.1 all-gather.4
  59.5 43.9 all-gather.6
  105.2 278.3 all-gather.8
  385.8 99.5 all-reduce.1
  503.2 76.7 reduce-scatter.4
  583.2 76.2 reduce-scatter.2
